TPU v7x, 512 devices: a whole 4x8x8 slice. The times are simulated.
512 devices in a mesh: group: 8 (over y), dev: 64 (over x, z, core).
Axes of the slice: x: 4, y: 8, z: 8, core: 2. Of those that a mesh axis runs over, the one named last changes fastest.
Arguments:
- embeddings: float32 [524288, 256], P(('group', 'dev')), may hold values from -1.5 to 1.5
- adagrad_state: float32 [524288], P(('group', 'dev')), may hold values from 0.001 to 0.1
- relations: float32 [4, 256], replicated, may hold values from 0.1 to 1.9
- src_rows: int32 [2, 524288], P(None, ('group', 'dev')), may hold values from 0 to 1023
- rel_ids: int32 [2, 524288], P(None, ('group', 'dev')), may hold values from 0 to 3
- dst_slots: int32 [2, 524288], P(None, ('group', 'dev')), may hold values from 0 to 2047
- live_counts: int32 [2, 512], P(None, ('group', 'dev')), may hold values from 1 to 1024, 174592 in all within a row
- request_rows: int32 [2, 1048576], P(None, ('group', 'dev')), may hold values from 0 to 1023
Outputs:
- updated_embeddings: float32 [524288, 256], P(('group', 'dev'))
- updated_state: float32 [524288], P(('group', 'dev'))
Inputs may be any that keep to these rules, and one draw needn't show every extreme that they name: `live_counts`: in every bucket one device has exactly 1024 live edges, and the live edges of all devices sum to the same total in every bucket.
All inputs are finite; a program needn't handle non-finite values.
Results may differ from a plain program's by a relative error of at most 0.0034.
Values may be sent and summed in bfloat16 or wider, within the bound.
A program may use at most 64 MiB of HBM per device.

v0:
```python
import jax
import jax.numpy as jnp
from jax import lax
from jax.sharding import PartitionSpec as P

learn_rate = 0.1
adagrad_eps = 1e-10


def shifted(x, axis, by):
    devices = lax.axis_size(axis)
    return lax.ppermute(x, axis, [(i, (i + by) % devices) for i in range(devices)])


def edge_terms(current, fetched, relations, sources, relation_ids, targets, live_total):
    edge_slots = sources.shape[0]
    fetch_rows = fetched.shape[0]
    picks = (relation_ids[:, None] == jnp.arange(relations.shape[0])[None, :]).astype(jnp.float32)
    rel_rows = jnp.dot(picks, relations, precision=lax.Precision.HIGHEST)
    queries = (jnp.take(current, sources, axis=0) * rel_rows).astype(jnp.bfloat16)
    scores = lax.dot_general(
        queries, fetched, (((1,), (1,)), ((), ())), preferred_element_type=jnp.float32
    )
    target_hit = targets[:, None] == jnp.arange(fetch_rows)[None, :]
    positive = jnp.sum(jnp.where(target_hit, scores, 0.0), axis=1)
    live_mask = (jnp.arange(edge_slots) < live_total).astype(jnp.float32)
    coefficient = live_mask[:, None] * jax.nn.sigmoid(scores) / fetch_rows
    pulled = live_mask * jax.nn.sigmoid(-positive)
    coefficient = coefficient - jnp.where(target_hit, pulled[:, None], 0.0)
    coefficient = coefficient.astype(jnp.bfloat16)
    grad_query = jnp.dot(coefficient, fetched, preferred_element_type=jnp.float32)
    grad_fetched = lax.dot_general(
        coefficient, queries, (((0,), (0,)), ((), ())), preferred_element_type=jnp.float32
    )
    source_grads = jax.ops.segment_sum(
        grad_query * rel_rows, sources, num_segments=current.shape[0]
    )
    return (source_grads, grad_fetched)


def on_device(
    embeddings, adagrad_state, relations, src_rows, rel_ids, dst_slots, live_counts, request_rows
):
    groups = lax.axis_size("group")
    dev_count = lax.axis_size("dev")
    columns = embeddings.shape[1]
    own_rows = embeddings.shape[0]
    fetch_rows = request_rows.shape[1]
    per_owner = fetch_rows // dev_count
    current = embeddings
    row_state = adagrad_state
    for bucket in range(src_rows.shape[0]):
        offset = 1 + bucket % (groups - 1)
        back_by = groups - offset
        rounded = current.astype(jnp.bfloat16)
        request_ids = request_rows[bucket].reshape(dev_count, per_owner)
        incoming_ids = lax.all_to_all(request_ids, "dev", split_axis=0, concat_axis=0, tiled=True)
        mirror = shifted(rounded, "group", offset)
        served = jnp.take(mirror, incoming_ids.reshape(fetch_rows), axis=0)
        fetched = lax.all_to_all(
            served.reshape(dev_count, per_owner, columns),
            "dev",
            split_axis=0,
            concat_axis=0,
            tiled=True,
        ).reshape(fetch_rows, columns)
        source_grads, fetched_grads = edge_terms(
            current,
            fetched,
            relations,
            src_rows[bucket],
            rel_ids[bucket],
            dst_slots[bucket],
            live_counts[bucket, 0],
        )
        returned = lax.all_to_all(
            fetched_grads.reshape(dev_count, per_owner, columns),
            "dev",
            split_axis=0,
            concat_axis=0,
            tiled=True,
        )
        dense_grads = jax.ops.segment_sum(
            returned.reshape(fetch_rows, columns),
            incoming_ids.reshape(fetch_rows),
            num_segments=own_rows,
        )
        dest_grads = shifted(dense_grads, "group", back_by)
        grads = source_grads + dest_grads
        square = jnp.mean(grads * grads, axis=1)
        row_state = row_state + square
        current = current - learn_rate * grads / (jnp.sqrt(row_state)[:, None] + adagrad_eps)
    return (current, row_state)


def solution(mesh):
    return jax.shard_map(
        on_device,
        mesh=mesh,
        in_specs=(
            P(("group", "dev"), None),
            P(("group", "dev")),
            P(),
            P(None, ("group", "dev")),
            P(None, ("group", "dev")),
            P(None, ("group", "dev")),
            P(None, ("group", "dev")),
            P(None, ("group", "dev")),
        ),
        out_specs=(P(("group", "dev"), None), P(("group", "dev"))),
        check_vma=False,
    )
```

profile of v0, /device:TPU:1, one launch (start us, length us, event | category | flops | bytes accessed | tf_op | source)
XLA Modules:
  0.0 400.5 jit_solution(3636702420903475320)
XLA Ops:
  0.7 1.4 convert_element_type.36
  2.0 4.0 %collective-permute-start = (bf16[1024,256]{1,0:T(8,128)(2,1)S(1)}, bf16[1024,256]{1,0:T(8,128)(2,1)S(1)}, u32[]{:S(2)}, u32[]{:S(2)}) collective-permute-start(bf16[1024,256]{1,0:T(8,128)(2,1)S(1)} %convert_element_type.36), channel_id=1, source_target_pairs={{0,64},{64,128},{128,192},{192,256},{256,320},{320,384},{384,448},... | collective-permute-start | bytes 1572872 | tf_op jit(solution)/shard_map/ppermute | solution.py:12
  6.1 0.8 slice_reduce_fusion
  7.0 23.4 %all_to_all.38 = s32[64,1,32]{2,1,0:T(1,128)S(1)} all-to-all(s32[64,1,32]{2,1,0:T(1,128)S(1)} %bitcast.38), channel_id=1, replica_groups=mesh['group'=8,'dev'=64] {'dev'}, dimensions={0} | all-to-all | bytes 16384 | tf_op jit(solution)/shard_map/all_to_all | solution.py:57
  30.9 0.7 reduce.14
  31.7 7.5 %gather_fusion.1 = bf16[2048,256]{1,0:T(8,128)(2,1)S(1)} fusion(bf16[1024,256]{1,0:T(8,128)(2,1)S(1)} %collective-permute-done, s32[2048]{0:T(1024)S(1)} %fusion.10), kind=kCustom, calls=%fused_computation.1.clone | custom fusion | bytes 2105344 | tf_op jit(solution)/shard_map/jit(_take)/gather | solution.py:59
  39.3 1.3 broadcast_select_fusion.1
  40.5 4.8 %all-to-all-start.1 = ((bf16[64,32,256]{2,1,0:T(8,128)(2,1)}), bf16[64,32,256]{2,1,0:T(8,128)(2,1)S(1)}, u32[]{:S(2)}, u32[]{:S(2)}) async-start(bf16[64,32,256]{2,1,0:T(8,128)(2,1)} %bitcast.4), calls=%async_computation.1 | async-start | bytes 2097152 | tf_op jit(solution)/shard_map/all_to_all | solution.py:60
  45.3 3.5 gather_fusion
  48.8 0.6 fusion.20
  49.4 0.7 fusion.13
  50.2 2.1 fusion.1
  52.3 21.5 %all-to-all-done.1 = bf16[64,32,256]{2,1,0:T(8,128)(2,1)S(1)} async-done(((bf16[64,32,256]{2,1,0:T(8,128)(2,1)}), bf16[64,32,256]{2,1,0:T(8,128)(2,1)S(1)}, u32[]{:S(2)}, u32[]{:S(2)}) %all-to-all-start.1) | async-done | bytes 1048608 | tf_op jit(solution)/shard_map/all_to_all | solution.py:60
  73.8 2.9 select_reduce_fusion.1
  76.8 0.8 divide_select_fusion.1
  77.6 3.6 subtract_convert_fusion.1
  81.1 1.9 copy-done.2
  83.1 1.4 fusion.21
  84.4 57.4 %all_to_all.39 = f32[64,32,256]{2,1,0:T(8,128)} all-to-all(f32[64,32,256]{2,1,0:T(8,128)S(1)} %bitcast.34), channel_id=1, replica_groups=mesh['group'=8,'dev'=64] {'dev'}, dimensions={0} | all-to-all | bytes 4194304 | tf_op jit(solution)/shard_map/all_to_all | solution.py:76
  141.9 13.0 %scatter_custom_fusion = f32[1024,256]{1,0:T(8,128)} fusion(s32[2048]{0:T(1024)S(1)} %reshape.132, f32[2048,256]{1,0:T(8,128)} %bitcast.33, f32[]{:T(128)} %constant.22.clone.1), kind=kCustom, calls=%fused_computation.30 | custom fusion | flops 524288 | bytes 1049088 | tf_op jit(solution)/shard_map/scatter-add | solution.py:83
  154.8 3.7 collective-permute-start.1
  158.5 4.7 %convolution_multiply_fusion.1 = f32[1024,256]{1,0:T(8,128)} fusion(f32[1024,256]{1,0:T(8,128)S(1)} %copy-done.4, bf16[1024,2048]{1,0:T(8,128)(2,1)} %copy-done.2, bf16[2048,256]{1,0:T(8,128)(2,1)} %bitcast.37), kind=kOutput, calls=%fused_computation.15 | convolution fusion | flops 1074003968 | bytes 7340032 | tf_op jit(solution)/shard_map/dot_general | solution.py:31
  163.3 18.0 %collective-permute-done.1 = f32[1024,256]{1,0:T(8,128)S(1)} collective-permute-done((f32[1024,256]{1,0:T(8,128)}, f32[1024,256]{1,0:T(8,128)S(1)}, u32[]{:S(2)}, u32[]{:S(2)}) %collective-permute-start.1) | collective-permute-done | bytes 1048608 | tf_op jit(solution)/shard_map/ppermute | solution.py:12
  181.2 6.9 %scatter_fusion = f32[1024,256]{1,0:T(8,128)S(1)} fusion(f32[1024,256]{1,0:T(8,128)S(1)} %collective-permute-done.1, s32[1024]{0:T(1024)S(1)} %bitcast.45, f32[1024,256]{1,0:T(8,128)} %convolution_multiply_fusion.1), kind=kCustom, calls=%fused_computation.5 | custom fusion | flops 262144 | bytes 3149824 | tf_op jit(solution)/shard_map/scatter-add | solution.py:35
  188.4 1.0 fusion.16
  189.4 5.6 %collective-permute-start.2 = (bf16[1024,256]{1,0:T(8,128)(2,1)}, bf16[1024,256]{1,0:T(8,128)(2,1)S(1)}, u32[]{:S(2)}, u32[]{:S(2)}) collective-permute-start(bf16[1024,256]{1,0:T(8,128)(2,1)} %get-tuple-element.8), channel_id=1, source_target_pairs={{0,128},{64,192},{128,256},{192,320},{256,384},{320,448},{384,0},{... | collective-permute-start | bytes 1572872 | tf_op jit(solution)/shard_map/ppermute | solution.py:12
  195.1 15.0 %all_to_all.40 = s32[64,1,32]{2,1,0:T(1,128)S(1)} all-to-all(s32[64,1,32]{2,1,0:T(1,128)S(1)} %bitcast.39), channel_id=1, replica_groups=mesh['group'=8,'dev'=64] {'dev'}, dimensions={0} | all-to-all | bytes 16384 | tf_op jit(solution)/shard_map/all_to_all | solution.py:57
  210.1 0.7 reduce.15
  211.0 7.5 %gather_fusion.3 = bf16[2048,256]{1,0:T(8,128)(2,1)S(1)} fusion(bf16[1024,256]{1,0:T(8,128)(2,1)S(1)} %collective-permute-done.2, s32[2048]{0:T(1024)S(1)} %fusion.11), kind=kCustom, calls=%fused_computation.3.clone | custom fusion | bytes 2105344 | tf_op jit(solution)/shard_map/jit(_take)/gather | solution.py:59
  218.5 1.2 broadcast_select_fusion
  219.7 12.9 %all-to-all-start.4 = ((bf16[64,32,256]{2,1,0:T(8,128)(2,1)}), bf16[64,32,256]{2,1,0:T(8,128)(2,1)}, u32[]{:S(2)}, u32[]{:S(2)}) async-start(bf16[64,32,256]{2,1,0:T(8,128)(2,1)} %bitcast.13), calls=%async_computation.4 | async-start | bytes 2097152 | tf_op jit(solution)/shard_map/all_to_all | solution.py:60
  233.2 0.6 fusion.7
  233.8 3.5 gather_fusion.2
  237.3 1.0 fusion
  238.3 22.8 %all-to-all-done.4 = bf16[64,32,256]{2,1,0:T(8,128)(2,1)} async-done(((bf16[64,32,256]{2,1,0:T(8,128)(2,1)}), bf16[64,32,256]{2,1,0:T(8,128)(2,1)}, u32[]{:S(2)}, u32[]{:S(2)}) %all-to-all-start.4) | async-done | bytes 1048608 | tf_op jit(solution)/shard_map/all_to_all | solution.py:60
  261.1 3.1 select_reduce_fusion
  264.2 0.6 divide_select_fusion
  264.8 3.6 subtract_convert_fusion
  268.4 1.9 copy-done.3
  270.3 1.4 fusion.22
  271.7 57.4 %all_to_all.41 = f32[64,32,256]{2,1,0:T(8,128)} all-to-all(f32[64,32,256]{2,1,0:T(8,128)S(1)} %bitcast.35), channel_id=1, replica_groups=mesh['group'=8,'dev'=64] {'dev'}, dimensions={0} | all-to-all | bytes 4194304 | tf_op jit(solution)/shard_map/all_to_all | solution.py:76
  329.0 13.0 %scatter_custom_fusion.2 = f32[1024,256]{1,0:T(8,128)} fusion(s32[2048]{0:T(1024)S(1)} %reshape.148, f32[2048,256]{1,0:T(8,128)} %bitcast.32, f32[]{:T(128)} %constant.22.clone.1), kind=kCustom, calls=%fused_computation.28 | custom fusion | flops 524288 | bytes 1049088 | tf_op jit(solution)/shard_map/scatter-add | solution.py:83
  342.0 1.9 collective-permute-start.3
  343.9 4.7 %convolution_multiply_fusion = f32[1024,256]{1,0:T(8,128)} fusion(f32[1024,256]{1,0:T(8,128)S(1)} %fusion.7, bf16[1024,2048]{1,0:T(8,128)(2,1)} %copy-done.3, bf16[2048,256]{1,0:T(8,128)(2,1)} %bitcast.14), kind=kOutput, calls=%fused_computation.14 | convolution fusion | flops 1074003968 | bytes 7340032 | tf_op jit(solution)/shard_map/dot_general | solution.py:31
  348.6 43.0 %collective-permute-done.3 = f32[1024,256]{1,0:T(8,128)S(1)} collective-permute-done((f32[1024,256]{1,0:T(8,128)}, f32[1024,256]{1,0:T(8,128)S(1)}, u32[]{:S(2)}, u32[]{:S(2)}) %collective-permute-start.3) | collective-permute-done | bytes 1048608 | tf_op jit(solution)/shard_map/ppermute | solution.py:12
  391.6 6.9 %scatter_fusion.1 = f32[1024,256]{1,0:T(8,128)S(1)} fusion(f32[1024,256]{1,0:T(8,128)S(1)} %collective-permute-done.3, s32[1024]{0:T(1024)S(1)} %bitcast.42, f32[1024,256]{1,0:T(8,128)} %convolution_multiply_fusion), kind=kCustom, calls=%fused_computation.7 | custom fusion | flops 262144 | bytes 3149824 | tf_op jit(solution)/shard_map/scatter-add | solution.py:35
  398.8 0.6 sqrt_add_fusion
  399.4 1.2 divide_subtract_fusion
  (46 shorter events, 1.9 us)
Async XLA Ops:
  0.6 49.5 %copy-start = (f32[4,256]{1,0:T(4,128)S(1)}, f32[4,256]{1,0:T(4,128)}, u32[]{:S(2)}) copy-start(f32[4,256]{1,0:T(4,128)} %param.14) | copy-start | bytes 12292
  0.6 44.7 %copy-start.1 = (f32[1024,256]{1,0:T(8,128)S(1)}, f32[1024,256]{1,0:T(8,128)}, u32[]{:S(2)}) copy-start(f32[1024,256]{1,0:T(8,128)} %param.12) | copy-start | bytes 3145732
  0.7 44.6 %copy-start.9 = (s32[2,1024]{1,0:T(2,128)S(1)}, s32[2,1024]{1,0:T(2,128)}, u32[]{:S(2)}) copy-start(s32[2,1024]{1,0:T(2,128)} %param.15) | copy-start | bytes 24580
  2.0 29.7 %collective-permute-start = (bf16[1024,256]{1,0:T(8,128)(2,1)S(1)}, bf16[1024,256]{1,0:T(8,128)(2,1)S(1)}, u32[]{:S(2)}, u32[]{:S(2)}) collective-permute-start(bf16[1024,256]{1,0:T(8,128)(2,1)S(1)} %convert_element_type.36), channel_id=1, source_target_pairs={{0,64},{64,128},{128,192},{192,256},{256,320},{320,384},{384,448},... | collective-permute-start | bytes 1572872 | tf_op jit(solution)/shard_map/ppermute | solution.py:12
  39.2 9.6 %copy-start.12 = (s32[2,1]{0,1:T(1,128)S(1)}, s32[2,1]{0,1:T(1,128)}, u32[]{:S(2)}) copy-start(s32[2,1]{0,1:T(1,128)} %param.18) | copy-start | bytes 28
  39.2 10.9 %copy-start.10 = (s32[2,1024]{1,0:T(2,128)S(1)}, s32[2,1024]{1,0:T(2,128)}, u32[]{:S(2)}) copy-start(s32[2,1024]{1,0:T(2,128)} %param.16) | copy-start | bytes 24580
  39.2 10.9 %copy-start.11 = (s32[2,1024]{1,0:T(2,128)S(1)}, s32[2,1024]{1,0:T(2,128)}, u32[]{:S(2)}) copy-start(s32[2,1024]{1,0:T(2,128)} %param.17) | copy-start | bytes 24580
  40.5 33.3 %all-to-all-start.1 = ((bf16[64,32,256]{2,1,0:T(8,128)(2,1)}), bf16[64,32,256]{2,1,0:T(8,128)(2,1)S(1)}, u32[]{:S(2)}, u32[]{:S(2)}) async-start(bf16[64,32,256]{2,1,0:T(8,128)(2,1)} %bitcast.4), calls=%async_computation.1 | async-start | bytes 2097152 | tf_op jit(solution)/shard_map/all_to_all | solution.py:60
  73.8 7.3 %copy-start.5 = (bf16[64,32,256]{2,1,0:T(8,128)(2,1)}, bf16[64,32,256]{2,1,0:T(8,128)(2,1)S(1)}, u32[]{:S(2)}) copy-start(bf16[64,32,256]{2,1,0:T(8,128)(2,1)S(1)} %all-to-all-done.1) | copy-start | bytes 3145732
  76.8 6.3 %copy-start.6 = (bf16[1024,256]{1,0:T(8,128)(2,1)S(1)}, bf16[1024,256]{1,0:T(8,128)(2,1)}, u32[]{:S(2)}) copy-start(bf16[1024,256]{1,0:T(8,128)(2,1)} %get-tuple-element.18) | copy-start | bytes 1572868
  81.1 1.9 copy-start.2
  83.1 75.5 %copy-start.4 = (f32[1024,256]{1,0:T(8,128)S(1)}, f32[1024,256]{1,0:T(8,128)}, u32[]{:S(2)}) copy-start(f32[1024,256]{1,0:T(8,128)} %get-tuple-element.19) | copy-start | bytes 3145732
  154.8 26.4 %collective-permute-start.1 = (f32[1024,256]{1,0:T(8,128)}, f32[1024,256]{1,0:T(8,128)S(1)}, u32[]{:S(2)}, u32[]{:S(2)}) collective-permute-start(f32[1024,256]{1,0:T(8,128)} %scatter_custom_fusion), channel_id=1, source_target_pairs={{0,448},{64,0},{128,64},{192,128},{256,192},{320,256},{384,320},{4... | collective-permute-start | bytes 3145736 | tf_op jit(solution)/shard_map/ppermute | solution.py:12
  163.3 25.1 %copy-start.8 = (f32[1024]{0:T(1024)S(1)}, f32[1024]{0:T(1024)}, u32[]{:S(2)}) copy-start(f32[1024]{0:T(1024)} %param.13) | copy-start | bytes 12292
  189.4 21.5 %collective-permute-start.2 = (bf16[1024,256]{1,0:T(8,128)(2,1)}, bf16[1024,256]{1,0:T(8,128)(2,1)S(1)}, u32[]{:S(2)}, u32[]{:S(2)}) collective-permute-start(bf16[1024,256]{1,0:T(8,128)(2,1)} %get-tuple-element.8), channel_id=1, source_target_pairs={{0,128},{64,192},{128,256},{192,320},{256,384},{320,448},{384,0},{... | collective-permute-start | bytes 1572872 | tf_op jit(solution)/shard_map/ppermute | solution.py:12
  219.7 41.4 %all-to-all-start.4 = ((bf16[64,32,256]{2,1,0:T(8,128)(2,1)}), bf16[64,32,256]{2,1,0:T(8,128)(2,1)}, u32[]{:S(2)}, u32[]{:S(2)}) async-start(bf16[64,32,256]{2,1,0:T(8,128)(2,1)} %bitcast.13), calls=%async_computation.4 | async-start | bytes 2097152 | tf_op jit(solution)/shard_map/all_to_all | solution.py:60
  264.2 6.1 %copy-start.7 = (bf16[1024,256]{1,0:T(8,128)(2,1)S(1)}, bf16[1024,256]{1,0:T(8,128)(2,1)}, u32[]{:S(2)}) copy-start(bf16[1024,256]{1,0:T(8,128)(2,1)} %fusion) | copy-start | bytes 1572868
  268.4 1.9 copy-start.3
  342.0 49.6 %collective-permute-start.3 = (f32[1024,256]{1,0:T(8,128)}, f32[1024,256]{1,0:T(8,128)S(1)}, u32[]{:S(2)}, u32[]{:S(2)}) collective-permute-start(f32[1024,256]{1,0:T(8,128)} %scatter_custom_fusion.2), channel_id=1, source_target_pairs={{0,384},{64,448},{128,0},{192,64},{256,128},{320,192},{384,256},{4... | collective-permute-start | bytes 3145736 | tf_op jit(solution)/shard_map/ppermute | solution.py:12
where the time goes:
time: 403 us; the launch traced here: 401 us
  blocking collectives  153 us (38%)
  waiting for transfers between devices  105 us (26%)
  other arithmetic  59.1 us (15%)
  starting transfers between devices  32.9 us (8%)
  local copies, waits for them, and re-layouts  28.1 us (7%)
  matrix products  21 us (5%)
    all_to_all x2, blocking collectives, on_device(): lax.all_to_all(fetched_grads.reshape(dev_count, per_owner, columns), 'dev...  115 us
    ppermute x4, waiting for transfers between devices, shifted(): lax.ppermute(x, axis, [(i, (i + by) % devices) for i in range(devices)])  60.9 us
    all_to_all x2, waiting for transfers between devices, on_device(): lax.all_to_all(served.reshape(dev_count, per_owner, columns), 'dev', spli...  44.3 us
    all_to_all x2, blocking collectives, on_device(): lax.all_to_all(request_ids, 'dev', split_axis=0, concat_axis=0, tiled=True)  38.4 us
    scatter-add x2, other arithmetic, on_device(): jax.ops.segment_sum(returned.reshape(fetch_rows, columns), incoming_ids.r...  25.9 us
    all_to_all x2, starting transfers between devices, on_device(): lax.all_to_all(served.reshape(dev_count, per_owner, columns), 'dev', spli...  17.6 us
    ppermute x4, starting transfers between devices, shifted(): lax.ppermute(x, axis, [(i, (i + by) % devices) for i in range(devices)])  15.2 us
    gather x2, local copies, waits for them, and re-layouts, on_device(): served = jnp.take(mirror, incoming_ids.reshape(fetch_rows), axis=0)  15 us
  transfers between devices with their start and end apart: 6, of which 4 were waited for; matrix products, arithmetic and copies ran while one was open for 6% of the time, Pallas kernels for 0%

commit v1 on v0

v1 whole, which is shorter than its diff:
```python
import functools

import jax
import jax.numpy as jnp
from jax import lax
from jax.experimental import pallas as pl
from jax.experimental.pallas import tpu as pltpu
from jax.sharding import PartitionSpec as P

MESH = pl.DeviceIdType.MESH
learn_rate = 0.1
adagrad_eps = 1e-10

NX, NZ, NC = 4, 8, 2
PEERS = NX * NZ * NC
ROWS, DIM = 1024, 256
EDGES, FETCH = 1024, 2048
CAP = FETCH // PEERS
STEP = 256
SLOTS = STEP // CAP
STEPS = FETCH // STEP
TILE = 256
BF16, F32 = jnp.bfloat16, jnp.float32


def disp(j):
    a, b = j // NZ, j % NZ
    u = (a + b) % (NX * NC)
    return u // NC, b, u % NC


def column(row):
    return jnp.broadcast_to(row, (128, 128)).T


def lanes(shape, start=0):
    return lax.broadcasted_iota(jnp.int32, shape, 1) + start


def subs(shape, start=0):
    return lax.broadcasted_iota(jnp.int32, shape, 0) + start


def one_hot_rows(rows):
    tiles = []
    for row in rows:
        col = column(row)
        tiles.append(
            jnp.concatenate(
                [(col == lanes((128, 128), 128 * t)).astype(F32).astype(BF16) for t in range(ROWS // 128)], axis=1
            )
        )
    return jnp.concatenate(tiles, axis=0)


def one_hot_columns(rows, start, count):
    place = subs((count, 128), start)
    return jnp.concatenate(
        [(place == jnp.broadcast_to(row, (count, 128))).astype(F32).astype(BF16) for row in rows], axis=1
    )


def dot(a, b, dims=((1,), (0,))):
    return lax.dot_general(a, b, (dims, ((), ())), preferred_element_type=F32)


def kernel(
    offsets,
    table_in, state_in, relations, src_ref, rel_ref, dst_ref, live_ref, request_ref,
    table, state_out,
    state, split, relrow, query, dstcol, gradq, total,
    ask, asked, packed,
    served, fetched, gradf, returned,
    ask_sent, ask_here, serve_sent, serve_here, return_sent, return_here,
):
    groups = lax.axis_size("group")
    g, d = lax.axis_index("group"), lax.axis_index("dev")
    mx, mz, mc = d // (NZ * NC), (d // NC) % NZ, d % NC

    def toward(j):
        x, z, c = disp(j)
        return ((mx + x) % NX) * (NZ * NC) + ((mz + z) % NZ) * NC + (mc + c) % NC

    def back(j):
        x, z, c = disp(j)
        return ((mx + NX - x) % NX) * (NZ * NC) + ((mz + NZ - z) % NZ) * NC + (mc + NC - c) % NC

    def rows_of(ref, j):
        return ref.at[pl.ds(pl.multiple_of(j * CAP, CAP), CAP)]

    def send(src, dst, sent, here, group, dev):
        pltpu.make_async_remote_copy(
            src_ref=src, dst_ref=dst, send_sem=sent, recv_sem=here, device_id=(group, dev), device_id_type=MESH
        ).start()

    def landed(ref, sem):
        pltpu.make_async_copy(ref, ref, sem).wait()

    barrier = pltpu.get_barrier_semaphore()

    def greet(j, carry):
        for s in offsets:
            for other in (s, groups - s):
                pl.semaphore_signal(barrier, 1, device_id=((g + other) % groups, j), device_id_type=MESH)
        return carry

    lax.fori_loop(0, PEERS, greet, 0)

    for b in range(len(offsets)):
        for r in range(FETCH // 128):
            row = request_ref[b : b + 1, 128 * r : 128 * (r + 1)]
            for u in range(4):
                turned = row if u == 0 else jnp.concatenate([row[:, 128 - CAP * u :], row[:, : 128 - CAP * u]], axis=1)
                ask[b, u, r] = turned

    pl.semaphore_wait(barrier, 2 * PEERS * len(offsets))

    for b, s in enumerate(offsets):

        def ask_owner(j, carry):
            owner = back(j)
            turn = (j % 4 + 4 - owner % 4) % 4
            send(
                ask.at[b, turn, owner // 4], asked.at[b, j], ask_sent.at[b], ask_here.at[b], (g + groups - s) % groups, owner
            )
            return carry

        lax.fori_loop(0, PEERS, ask_owner, 0)

    table[...] = table_in[...]
    for t in range(ROWS // 128):
        state[128 * t : 128 * (t + 1), :] = column(state_in[t : t + 1, :])

    for b, s in enumerate(offsets):
        ahead, behind = (g + s) % groups, (g + groups - s) % groups

        high = table[...].astype(BF16)
        split[:, :DIM] = high
        split[:, DIM:] = (table[...] - high.astype(F32)).astype(BF16)

        landed(asked.at[b], ask_here.at[b])
        lane = lanes((1, 128))
        for i in range(FETCH // 128):
            row = asked[b, 4 * i + 3]
            for m in (2, 1, 0):
                row = jnp.where(lane < CAP * (m + 1), asked[b, 4 * i + m], row)
            packed[b, i : i + 1, :] = row

        def serve(i, carry):
            ids = [packed[b, pl.ds(2 * i + h, 1), :] for h in range(2)]
            at = pl.ds(pl.multiple_of(i * STEP, STEP), STEP)
            served[b, at, :] = dot(one_hot_rows(ids), split[:, :DIM]).astype(BF16)

            def push(m, c):
                j = i * SLOTS + m
                send(
                    rows_of(served.at[b], j), rows_of(fetched.at[b], j), serve_sent.at[b], serve_here.at[b, i], ahead, toward(j)
                )
                return c

            lax.fori_loop(0, SLOTS, push, 0)
            return carry

        lax.fori_loop(0, STEPS, serve, 0)

        live = live_ref[b]
        edge = subs((EDGES // 128, 128)) * 128 + lanes((EDGES // 128, 128))
        source = jnp.where(edge < live, src_ref[b], -1)
        goal = dst_ref[b]
        owner = goal >> 5
        jz = (mz + NZ - ((owner >> 1) & (NZ - 1))) & (NZ - 1)
        ju = ((mx + NX - (owner >> 4)) & (NX - 1)) * NC + ((mc + NC - (owner & 1)) & 1)
        goal = ((((ju + NX * NC - jz) & (NX * NC - 1)) * NZ + jz) << 5) + (goal & (CAP - 1))
        kind = rel_ref[b]
        for t in range(EDGES // TILE):
            at = slice(t * TILE, (t + 1) * TILE)
            picks = [slice(2 * t + h, 2 * t + h + 1) for h in range(2)]
            rel = jnp.concatenate([column(kind[p, :]) for p in picks], axis=0)
            rel = jnp.concatenate([rel, rel], axis=1)
            wide = relations[0:1, :]
            for n in range(1, relations.shape[0]):
                wide = jnp.where(rel == n, relations[n : n + 1, :], wide)
            relrow[at, :] = wide
            both = dot(one_hot_rows([source[p, :] for p in picks]), split[...])
            query[at, :] = ((both[:, :DIM] + both[:, DIM:]) * wide).astype(BF16)
            dstcol[at, :] = jnp.concatenate([column(goal[p, :]) for p in picks], axis=0)
        gradq[...] = jnp.zeros_like(gradq)

        def score(i, carry):
            at = pl.ds(pl.multiple_of(i * STEP, STEP), STEP)
            landed(fetched.at[b, at], serve_here.at[b, i])
            rows = fetched[b, at, :]
            grads = jnp.zeros((STEP, DIM), F32)
            for t in range(EDGES // TILE):
                edges = slice(t * TILE, (t + 1) * TILE)
                q = query[edges, :]
                u = jnp.tanh(dot(q, rows, ((1,), (1,))) * 0.5)
                want = dstcol[edges, :] - i * STEP
                hit = jnp.concatenate([want == lanes((TILE, 128), 128 * h) for h in range(STEP // 128)], axis=1)
                a = 0.5 / FETCH
                coef = jnp.where(hit, u * (a + 0.5) + (a - 0.5), u * a + a).astype(BF16)
                gradq[edges, :] += dot(coef, rows)
                grads += dot(coef, q, ((0,), (0,)))
            gradf[b, at, :] = grads.astype(BF16)

            def push(m, c):
                j = i * SLOTS + m
                send(
                    rows_of(gradf.at[b], j), rows_of(returned.at[b], j), return_sent.at[b], return_here.at[b, i], behind, back(j)
                )
                return c

            lax.fori_loop(0, SLOTS, push, 0)
            return carry

        lax.fori_loop(0, STEPS, score, 0)

        whole = gradq[...] * relrow[...]
        top = whole.astype(BF16)
        parts = jnp.concatenate([top, (whole - top.astype(F32)).astype(BF16)], axis=1)
        for t in range(ROWS // TILE):
            at = slice(t * TILE, (t + 1) * TILE)
            spots = [source[r : r + 1, :] for r in range(EDGES // 128)]
            both = dot(one_hot_columns(spots, t * TILE, TILE), parts)
            total[at, :] = both[:, :DIM] + both[:, DIM:]

        def collect(i, carry):
            at = pl.ds(pl.multiple_of(i * STEP, STEP), STEP)
            landed(returned.at[b, at], return_here.at[b, i])
            ids = [packed[b, pl.ds(2 * i + h, 1), :] for h in range(2)]
            back_rows = returned[b, at, :]
            for t in range(ROWS // TILE):
                spot = slice(t * TILE, (t + 1) * TILE)
                total[spot, :] += dot(one_hot_columns(ids, t * TILE, TILE), back_rows)
            return carry

        lax.fori_loop(0, STEPS, collect, 0)

        for t in range(ROWS // TILE):
            at = slice(t * TILE, (t + 1) * TILE)
            grad = total[at, :]
            now = state[at, :] + jnp.mean(grad * grad, axis=1, keepdims=True)
            state[at, :] = now
            rate = learn_rate / (jnp.sqrt(now) + adagrad_eps)
            table[at, :] = table[at, :] - grad * jnp.concatenate([rate, rate], axis=1)

    for t in range(ROWS // 128):
        state_out[t : t + 1, :] = state[128 * t : 128 * (t + 1), :].T[0:1, :]

    for b in range(len(offsets)):
        landed(asked.at[b], ask_sent.at[b])
        landed(served.at[b], serve_sent.at[b])
        landed(gradf.at[b], return_sent.at[b])


def on_device(
    embeddings, adagrad_state, relations, src_rows, rel_ids, dst_slots, live_counts, request_rows
):
    groups = lax.axis_size("group")
    buckets = src_rows.shape[0]
    offsets = tuple(1 + b % (groups - 1) for b in range(buckets))
    blocks = (buckets, EDGES // 128, 128)
    vmem = pl.BlockSpec(memory_space=pltpu.VMEM)
    smem = pl.BlockSpec(memory_space=pltpu.SMEM)
    table, state = pl.pallas_call(
        functools.partial(kernel, offsets),
        out_shape=(
            jax.ShapeDtypeStruct((ROWS, DIM), F32),
            jax.ShapeDtypeStruct((ROWS // 128, 128), F32),
        ),
        in_specs=[vmem] * 6 + [smem, vmem],
        out_specs=(vmem, vmem),
        scratch_shapes=[
            pltpu.VMEM((ROWS, 128), F32),
            pltpu.VMEM((ROWS, 2 * DIM), BF16),
            pltpu.VMEM((EDGES, DIM), F32),
            pltpu.VMEM((EDGES, DIM), BF16),
            pltpu.VMEM((EDGES, 128), jnp.int32),
            pltpu.VMEM((EDGES, DIM), F32),
            pltpu.VMEM((ROWS, DIM), F32),
            pltpu.VMEM((buckets, 4, FETCH // 128, 1, 128), jnp.int32),
            pltpu.VMEM((buckets, PEERS, 1, 128), jnp.int32),
            pltpu.VMEM((buckets, FETCH // 128, 128), jnp.int32),
            pltpu.VMEM((buckets, FETCH, DIM), BF16),
            pltpu.VMEM((buckets, FETCH, DIM), BF16),
            pltpu.VMEM((buckets, FETCH, DIM), BF16),
            pltpu.VMEM((buckets, FETCH, DIM), BF16),
            pltpu.SemaphoreType.DMA((buckets,)),
            pltpu.SemaphoreType.DMA((buckets,)),
            pltpu.SemaphoreType.DMA((buckets,)),
            pltpu.SemaphoreType.DMA((buckets, STEPS)),
            pltpu.SemaphoreType.DMA((buckets,)),
            pltpu.SemaphoreType.DMA((buckets, STEPS)),
        ],
        compiler_params=pltpu.CompilerParams(
            collective_id=0, has_side_effects=True, vmem_limit_bytes=44 * 1024 * 1024
        ),
        name="bucket_pass",
    )(
        embeddings,
        adagrad_state.reshape(ROWS // 128, 128),
        relations,
        src_rows.reshape(blocks),
        rel_ids.reshape(blocks),
        dst_slots.reshape(blocks),
        live_counts.reshape(buckets),
        request_rows,
    )
    return table, state.reshape(ROWS)


def solution(mesh):
    return jax.shard_map(
        on_device,
        mesh=mesh,
        in_specs=(
            P(("group", "dev"), None),
            P(("group", "dev")),
            P(),
            P(None, ("group", "dev")),
            P(None, ("group", "dev")),
            P(None, ("group", "dev")),
            P(None, ("group", "dev")),
            P(None, ("group", "dev")),
        ),
        out_specs=(P(("group", "dev"), None), P(("group", "dev"))),
        check_vma=False,
    )
```

time: 403 us -> 174 us (0.43)
  Pallas kernels: 0 us -> 168 us
  blocking collectives: 153 us -> 0 us
  waiting for transfers between devices: 105 us -> 0 us
  other arithmetic: 59.1 us -> 0 us
  starting transfers between devices: 32.9 us -> 0 us
  local copies, waits for them, and re-layouts: 28.1 us -> 4.9 us
  matrix products: 21 us -> 0 us
    pallas_call x0 -> x1, Pallas kernels: none -> 168 us  [on_device(): pl.pallas_call(functools.partial(kernel, offsets), out_shape=(jax.ShapeDt...]
    all_to_all x4 -> x0, blocking collectives: 153 us -> none  [the longest x2 115 us: on_device(): lax.all_to_all(fetched_grads.reshape(dev_count, per_owner, columns), 'dev...]
    ppermute x4 -> x0, waiting for transfers between devices: 60.9 us -> none  [shifted(): lax.ppermute(x, axis, [(i, (i + by) % devices) for i in range(devices)])]
    all_to_all x2 -> x0, waiting for transfers between devices: 44.3 us -> none  [on_device(): lax.all_to_all(served.reshape(dev_count, per_owner, columns), 'dev', spli...]
    scatter-add x4 -> x0, other arithmetic: 39.8 us -> none  [the longest x2 25.9 us: on_device(): jax.ops.segment_sum(returned.reshape(fetch_rows, columns), incoming_ids.r...]
    gather x4 -> x0, local copies, waits for them, and re-layouts: 21.9 us -> none  [the longest x2 15 us: on_device(): served = jnp.take(mirror, incoming_ids.reshape(fetch_rows), axis=0)]
    dot_general x8 -> x0, matrix products: 21 us -> none  [the longest x2 9.46 us: edge_terms(): jnp.dot(coefficient, fetched, preferred_element_type=jnp.float32)]
    all_to_all x2 -> x0, starting transfers between devices: 17.6 us -> none  [on_device(): lax.all_to_all(served.reshape(dev_count, per_owner, columns), 'dev', spli...]
  transfers between devices with their start and end apart: 6 -> 0, of which waited for: 4 -> 0; matrix products, arithmetic and copies ran while one was open for 6% -> 0% of each run, Pallas kernels for 0% -> 0%
where the time goes in v1:
time: 174 us
  Pallas kernels  168 us (97%)
  local copies, waits for them, and re-layouts  4.9 us (3%)
    pallas_call x1, Pallas kernels, on_device(): pl.pallas_call(functools.partial(kernel, offsets), out_shape=(jax.ShapeDt...  168 us
    unnamed x19, local copies, waits for them, and re-layouts  4.9 us

profile of v1, /device:TPU:1, one launch (start us, length us, event | category | flops | bytes accessed | tf_op | source)
XLA Modules:
  0.0 173.9 jit_solution(1427286247691543033)
XLA Ops:
  0.6 0.0 copy-start.5
  0.6 0.7 copy-done.5
  1.3 0.0 copy-start.6
  1.3 0.0 copy-start.7
  1.3 0.7 copy-done.6
  2.0 0.0 copy-done.7
  2.0 0.0 copy-start.1
  2.0 0.0 copy-start.2
  2.0 0.0 copy-start.3
  2.1 0.0 copy-start.4
  2.1 0.7 copy-done.1
  2.8 0.0 copy-done.2
  2.8 0.0 copy-done.3
  2.8 0.0 copy-done.4
  2.8 0.0 copy-start
  2.8 1.2 copy-done
  4.0 168.3 %bucket_pass.1 = (f32[1024,256]{1,0:T(8,128)S(1)}, f32[8,128]{1,0:T(8,128)S(1)}) custom-call(f32[1024,256]{1,0:T(8,128)S(1)} %copy-done, f32[8,128]{1,0:T(8,128)S(1)} %bitcast.14, f32[4,256]{1,0:T(4,128)S(1)} %copy-done.3, s32[2,8,128]{2,1,0:T(8,128)S(1)} %bitcast.13, s32[2,8,128]{2,1,0:T(8,128)S(1)} %get-tuple-element.7.rel_ref, ...), custom_call_target="tpu_custom_call" | custom-call | tf_op jit(solution)/shard_map/bucket_pass/pallas_call | solution.py:265
  172.3 1.0 copy.19
  173.3 0.6 copy.20
  (2 shorter events, 0.0 us)
Async XLA Ops:
  0.6 0.7 copy-start.5
  1.3 0.7 copy-start.6
  1.3 0.7 copy-start.7
  2.0 0.7 copy-start.1
  2.0 0.7 copy-start.2
  2.0 0.7 copy-start.3
  2.1 0.7 copy-start.4
  2.8 1.2 copy-start

commit v2 on v1

--- a/solution.py
+++ b/solution.py
@@ -20,13 +20,14 @@
 SLOTS = STEP // CAP
 STEPS = FETCH // STEP
 TILE = 256
+LEADS = (3, 3)
+LAGS = (6, 0)
 BF16, F32 = jnp.bfloat16, jnp.float32
 
 
-def disp(j):
-    a, b = j // NZ, j % NZ
-    u = (a + b) % (NX * NC)
-    return u // NC, b, u % NC
+def disp(a, b):
+    u = (a + b) & (NX * NC - 1)
+    return u // NC if isinstance(u, int) else u >> 1, b, u & (NC - 1)
 
 
 def column(row):
@@ -77,13 +78,13 @@
     g, d = lax.axis_index("group"), lax.axis_index("dev")
     mx, mz, mc = d // (NZ * NC), (d // NC) % NZ, d % NC
 
-    def toward(j):
-        x, z, c = disp(j)
-        return ((mx + x) % NX) * (NZ * NC) + ((mz + z) % NZ) * NC + (mc + c) % NC
-
-    def back(j):
-        x, z, c = disp(j)
-        return ((mx + NX - x) % NX) * (NZ * NC) + ((mz + NZ - z) % NZ) * NC + (mc + NC - c) % NC
+    def toward(a, b):
+        x, z, c = disp(a, b)
+        return ((mx + x) & (NX - 1)) * (NZ * NC) + ((mz + z) & (NZ - 1)) * NC + ((mc + c) & (NC - 1))
+
+    def back(a, b):
+        x, z, c = disp(a, b)
+        return ((mx + NX - x) & (NX - 1)) * (NZ * NC) + ((mz + NZ - z) & (NZ - 1)) * NC + ((mc + NC - c) & (NC - 1))
 
     def rows_of(ref, j):
         return ref.at[pl.ds(pl.multiple_of(j * CAP, CAP), CAP)]
@@ -115,23 +116,27 @@
 
     pl.semaphore_wait(barrier, 2 * PEERS * len(offsets))
 
-    for b, s in enumerate(offsets):
-
-        def ask_owner(j, carry):
-            owner = back(j)
-            turn = (j % 4 + 4 - owner % 4) % 4
-            send(
-                ask.at[b, turn, owner // 4], asked.at[b, j], ask_sent.at[b], ask_here.at[b], (g + groups - s) % groups, owner
-            )
+    def ask_owners(b):
+        behind = (g + groups - offsets[b]) % groups
+
+        def some(a, carry):
+            for m in range(NZ):
+                owner = back(a, m)
+                turn = (m + 4 - (owner & 3)) & 3
+                send(
+                    ask.at[b, turn, owner >> 2], asked.at[b, a * NZ + m], ask_sent.at[b], ask_here.at[b], behind, owner
+                )
             return carry
 
-        lax.fori_loop(0, PEERS, ask_owner, 0)
-
+        lax.fori_loop(0, PEERS // NZ, some, 0)
+
+    ask_owners(0)
     table[...] = table_in[...]
     for t in range(ROWS // 128):
         state[128 * t : 128 * (t + 1), :] = column(state_in[t : t + 1, :])
 
     for b, s in enumerate(offsets):
+        lead, lag = LEADS[b], LAGS[b]
         ahead, behind = (g + s) % groups, (g + groups - s) % groups
 
         high = table[...].astype(BF16)
@@ -146,22 +151,36 @@
                 row = jnp.where(lane < CAP * (m + 1), asked[b, 4 * i + m], row)
             packed[b, i : i + 1, :] = row
 
+        def push_served(i):
+            for m in range(SLOTS):
+                j = i * SLOTS + m
+                send(
+                    rows_of(served.at[b], j), rows_of(fetched.at[b], j), serve_sent.at[b], serve_here.at[b, i], ahead, toward(i, m)
+                )
+
+        def push_grads(i):
+            for m in range(SLOTS):
+                j = i * SLOTS + m
+                send(
+                    rows_of(gradf.at[b], j), rows_of(returned.at[b], j), return_sent.at[b], return_here.at[b, i], behind, back(i, m)
+                )
+
         def serve(i, carry):
             ids = [packed[b, pl.ds(2 * i + h, 1), :] for h in range(2)]
             at = pl.ds(pl.multiple_of(i * STEP, STEP), STEP)
             served[b, at, :] = dot(one_hot_rows(ids), split[:, :DIM]).astype(BF16)
 
-            def push(m, c):
-                j = i * SLOTS + m
-                send(
-                    rows_of(served.at[b], j), rows_of(fetched.at[b], j), serve_sent.at[b], serve_here.at[b, i], ahead, toward(j)
-                )
-                return c
-
-            lax.fori_loop(0, SLOTS, push, 0)
+
+            @pl.when(i < lead)
+            def _():
+                push_served(i)
+
             return carry
 
         lax.fori_loop(0, STEPS, serve, 0)
+
+        if b + 1 < len(offsets):
+            ask_owners(b + 1)
 
         live = live_ref[b]
         edge = subs((EDGES // 128, 128)) * 128 + lanes((EDGES // 128, 128))
@@ -189,6 +208,11 @@
         def score(i, carry):
             at = pl.ds(pl.multiple_of(i * STEP, STEP), STEP)
             landed(fetched.at[b, at], serve_here.at[b, i])
+
+            @pl.when(i + lead < STEPS)
+            def _():
+                push_served(i + lead)
+
             rows = fetched[b, at, :]
             grads = jnp.zeros((STEP, DIM), F32)
             for t in range(EDGES // TILE):
@@ -203,17 +227,16 @@
                 grads += dot(coef, q, ((0,), (0,)))
             gradf[b, at, :] = grads.astype(BF16)
 
-            def push(m, c):
-                j = i * SLOTS + m
-                send(
-                    rows_of(gradf.at[b], j), rows_of(returned.at[b], j), return_sent.at[b], return_here.at[b, i], behind, back(j)
-                )
-                return c
-
-            lax.fori_loop(0, SLOTS, push, 0)
+
+            @pl.when(i >= lag)
+            def _():
+                push_grads(i - lag)
+
             return carry
 
         lax.fori_loop(0, STEPS, score, 0)
+        for i in range(STEPS - lag, STEPS):
+            push_grads(i)
 
         whole = gradq[...] * relrow[...]
         top = whole.astype(BF16)

time: 174 us -> 158 us (0.908); the launches traced: 174 us -> 156 us
  Pallas kernels: 168 us -> 150 us
    pallas_call x1, Pallas kernels: 168 us -> 150 us  [on_device(): pl.pallas_call(functools.partial(kernel, offsets), out_shape=(jax.ShapeDt...]
where the time goes in v2:
time: 158 us; the launch traced here: 156 us
  Pallas kernels  150 us (95%)
  local copies, waits for them, and re-layouts  4.9 us (3%)
    pallas_call x1, Pallas kernels, on_device(): pl.pallas_call(functools.partial(kernel, offsets), out_shape=(jax.ShapeDt...  150 us
    unnamed x19, local copies, waits for them, and re-layouts  4.9 us

profile of v2, /device:TPU:1, one launch (start us, length us, event | category | flops | bytes accessed | tf_op | source)
XLA Modules:
  0.0 156.0 jit_solution(408929029602611770)
XLA Ops:
  0.6 0.0 copy-start.5
  0.6 0.7 copy-done.5
  1.3 0.0 copy-start.6
  1.3 0.0 copy-start.7
  1.3 0.7 copy-done.6
  2.0 0.0 copy-done.7
  2.0 0.0 copy-start.1
  2.0 0.0 copy-start.2
  2.0 0.0 copy-start.3
  2.1 0.0 copy-start.4
  2.1 0.7 copy-done.1
  2.8 0.0 copy-done.2
  2.8 0.0 copy-done.3
  2.8 0.0 copy-done.4
  2.8 0.0 copy-start
  2.8 1.2 copy-done
  4.0 150.4 %bucket_pass.1 = (f32[1024,256]{1,0:T(8,128)S(1)}, f32[8,128]{1,0:T(8,128)S(1)}) custom-call(f32[1024,256]{1,0:T(8,128)S(1)} %copy-done, f32[8,128]{1,0:T(8,128)S(1)} %bitcast.14, f32[4,256]{1,0:T(4,128)S(1)} %copy-done.3, s32[2,8,128]{2,1,0:T(8,128)S(1)} %bitcast.13, s32[2,8,128]{2,1,0:T(8,128)S(1)} %get-tuple-element.7.rel_ref, ...), custom_call_target="tpu_custom_call" | custom-call | tf_op jit(solution)/shard_map/bucket_pass/pallas_call | solution.py:288
  154.4 1.0 copy.19
  155.4 0.6 copy.20
  (2 shorter events, 0.0 us)
Async XLA Ops:
  0.6 0.7 copy-start.5
  1.3 0.7 copy-start.6
  1.3 0.7 copy-start.7
  2.0 0.7 copy-start.1
  2.0 0.7 copy-start.2
  2.0 0.7 copy-start.3
  2.1 0.7 copy-start.4
  2.8 1.2 copy-start

commit v3 on v2

--- a/solution.py
+++ b/solution.py
@@ -21,7 +21,7 @@
 STEPS = FETCH // STEP
 TILE = 256
 LEADS = (3, 3)
-LAGS = (6, 0)
+LAGS = (5, 0)
 BF16, F32 = jnp.bfloat16, jnp.float32
 
 
@@ -67,8 +67,9 @@
 
 def kernel(
     offsets,
-    table_in, state_in, relations, src_ref, rel_ref, dst_ref, live_ref, request_ref,
+    table_in, state_in, relations_in, src_in, rel_in, dst_in, live_in, request_in,
     table, state_out,
+    relations, state_rows, src_ref, rel_ref, dst_ref, live_ref, request_ref, load_sem,
     state, split, relrow, query, dstcol, gradq, total,
     ask, asked, packed,
     served, fetched, gradf, returned,
@@ -105,7 +106,17 @@
                 pl.semaphore_signal(barrier, 1, device_id=((g + other) % groups, j), device_id_type=MESH)
         return carry
 
+    loads = [
+        pltpu.make_async_copy(src, dst, load_sem.at[n])
+        for n, (src, dst) in enumerate([
+            (request_in, request_ref), (table_in, table), (state_in, state_rows), (relations_in, relations),
+            (src_in, src_ref), (rel_in, rel_ref), (dst_in, dst_ref), (live_in, live_ref),
+        ])
+    ]
+    for load in loads:
+        load.start()
     lax.fori_loop(0, PEERS, greet, 0)
+    loads[0].wait()
 
     for b in range(len(offsets)):
         for r in range(FETCH // 128):
@@ -131,9 +142,10 @@
         lax.fori_loop(0, PEERS // NZ, some, 0)
 
     ask_owners(0)
-    table[...] = table_in[...]
+    for load in loads[1:]:
+        load.wait()
     for t in range(ROWS // 128):
-        state[128 * t : 128 * (t + 1), :] = column(state_in[t : t + 1, :])
+        state[128 * t : 128 * (t + 1), :] = column(state_rows[t : t + 1, :])
 
     for b, s in enumerate(offsets):
         lead, lag = LEADS[b], LAGS[b]
@@ -142,6 +154,38 @@
         high = table[...].astype(BF16)
         split[:, :DIM] = high
         split[:, DIM:] = (table[...] - high.astype(F32)).astype(BF16)
+
+        def queries():
+            live = jnp.broadcast_to(live_ref[0:1, b : b + 1], (EDGES // 128, 128))
+
+            def table_of(ref):
+                return jnp.concatenate([ref[b : b + 1, 128 * r : 128 * (r + 1)] for r in range(EDGES // 128)], axis=0)
+
+            edge = subs((EDGES // 128, 128)) * 128 + lanes((EDGES // 128, 128))
+            source = jnp.where(edge < live, table_of(src_ref), -1)
+            goal = table_of(dst_ref)
+            owner = goal >> 5
+            jz = (mz + NZ - ((owner >> 1) & (NZ - 1))) & (NZ - 1)
+            ju = ((mx + NX - (owner >> 4)) & (NX - 1)) * NC + ((mc + NC - (owner & 1)) & 1)
+            goal = ((((ju + NX * NC - jz) & (NX * NC - 1)) * NZ + jz) << 5) + (goal & (CAP - 1))
+            kind = table_of(rel_ref)
+            for t in range(EDGES // TILE):
+                at = slice(t * TILE, (t + 1) * TILE)
+                picks = [slice(2 * t + h, 2 * t + h + 1) for h in range(2)]
+                rel = jnp.concatenate([column(kind[p, :]) for p in picks], axis=0)
+                rel = jnp.concatenate([rel, rel], axis=1)
+                wide = relations[0:1, :]
+                for n in range(1, relations.shape[0]):
+                    wide = jnp.where(rel == n, relations[n : n + 1, :], wide)
+                relrow[at, :] = wide
+                both = dot(one_hot_rows([source[p, :] for p in picks]), split[...])
+                query[at, :] = ((both[:, :DIM] + both[:, DIM:]) * wide).astype(BF16)
+                dstcol[at, :] = jnp.concatenate([column(goal[p, :]) for p in picks], axis=0)
+            gradq[...] = jnp.zeros_like(gradq)
+            return source
+
+        if b == 0:
+            source = queries()
 
         landed(asked.at[b], ask_here.at[b])
         lane = lanes((1, 128))
@@ -179,31 +223,8 @@
 
         lax.fori_loop(0, STEPS, serve, 0)
 
-        if b + 1 < len(offsets):
-            ask_owners(b + 1)
-
-        live = live_ref[b]
-        edge = subs((EDGES // 128, 128)) * 128 + lanes((EDGES // 128, 128))
-        source = jnp.where(edge < live, src_ref[b], -1)
-        goal = dst_ref[b]
-        owner = goal >> 5
-        jz = (mz + NZ - ((owner >> 1) & (NZ - 1))) & (NZ - 1)
-        ju = ((mx + NX - (owner >> 4)) & (NX - 1)) * NC + ((mc + NC - (owner & 1)) & 1)
-        goal = ((((ju + NX * NC - jz) & (NX * NC - 1)) * NZ + jz) << 5) + (goal & (CAP - 1))
-        kind = rel_ref[b]
-        for t in range(EDGES // TILE):
-            at = slice(t * TILE, (t + 1) * TILE)
-            picks = [slice(2 * t + h, 2 * t + h + 1) for h in range(2)]
-            rel = jnp.concatenate([column(kind[p, :]) for p in picks], axis=0)
-            rel = jnp.concatenate([rel, rel], axis=1)
-            wide = relations[0:1, :]
-            for n in range(1, relations.shape[0]):
-                wide = jnp.where(rel == n, relations[n : n + 1, :], wide)
-            relrow[at, :] = wide
-            both = dot(one_hot_rows([source[p, :] for p in picks]), split[...])
-            query[at, :] = ((both[:, :DIM] + both[:, DIM:]) * wide).astype(BF16)
-            dstcol[at, :] = jnp.concatenate([column(goal[p, :]) for p in picks], axis=0)
-        gradq[...] = jnp.zeros_like(gradq)
+        if b > 0:
+            source = queries()
 
         def score(i, carry):
             at = pl.ds(pl.multiple_of(i * STEP, STEP), STEP)
@@ -238,6 +259,9 @@
         for i in range(STEPS - lag, STEPS):
             push_grads(i)
 
+        if b + 1 < len(offsets):
+            ask_owners(b + 1)
+
         whole = gradq[...] * relrow[...]
         top = whole.astype(BF16)
         parts = jnp.concatenate([top, (whole - top.astype(F32)).astype(BF16)], axis=1)
@@ -282,18 +306,25 @@
     groups = lax.axis_size("group")
     buckets = src_rows.shape[0]
     offsets = tuple(1 + b % (groups - 1) for b in range(buckets))
-    blocks = (buckets, EDGES // 128, 128)
     vmem = pl.BlockSpec(memory_space=pltpu.VMEM)
-    smem = pl.BlockSpec(memory_space=pltpu.SMEM)
+    hbm = pl.BlockSpec(memory_space=pltpu.HBM)
     table, state = pl.pallas_call(
         functools.partial(kernel, offsets),
         out_shape=(
             jax.ShapeDtypeStruct((ROWS, DIM), F32),
             jax.ShapeDtypeStruct((ROWS // 128, 128), F32),
         ),
-        in_specs=[vmem] * 6 + [smem, vmem],
+        in_specs=[hbm] * 8,
         out_specs=(vmem, vmem),
         scratch_shapes=[
+            pltpu.VMEM(relations.shape, F32),
+            pltpu.VMEM((ROWS // 128, 128), F32),
+            pltpu.VMEM((buckets, EDGES), jnp.int32),
+            pltpu.VMEM((buckets, EDGES), jnp.int32),
+            pltpu.VMEM((buckets, EDGES), jnp.int32),
+            pltpu.VMEM((1, buckets), jnp.int32),
+            pltpu.VMEM((buckets, FETCH), jnp.int32),
+            pltpu.SemaphoreType.DMA((8,)),
             pltpu.VMEM((ROWS, 128), F32),
             pltpu.VMEM((ROWS, 2 * DIM), BF16),
             pltpu.VMEM((EDGES, DIM), F32),
@@ -316,17 +347,17 @@
             pltpu.SemaphoreType.DMA((buckets, STEPS)),
         ],
         compiler_params=pltpu.CompilerParams(
-            collective_id=0, has_side_effects=True, vmem_limit_bytes=44 * 1024 * 1024
+            collective_id=0, has_side_effects=True, vmem_limit_bytes=62 * 1024 * 1024
         ),
         name="bucket_pass",
     )(
         embeddings,
         adagrad_state.reshape(ROWS // 128, 128),
         relations,
-        src_rows.reshape(blocks),
-        rel_ids.reshape(blocks),
-        dst_slots.reshape(blocks),
-        live_counts.reshape(buckets),
+        src_rows,
+        rel_ids,
+        dst_slots,
+        live_counts.reshape(1, buckets),
         request_rows,
     )
     return table, state.reshape(ROWS)

time: 158 us -> 157 us (level)
  the two profiles are of different devices: /device:TPU:1 before, /device:TPU:17 now
where the time goes in v3:
time: 157 us
  Pallas kernels  154 us (98%)
  local copies, waits for them, and re-layouts  2.86 us (2%)
    pallas_call x1, Pallas kernels, on_device(): pl.pallas_call(functools.partial(kernel, offsets), out_shape=(jax.ShapeDt...  154 us

profile of v3, /device:TPU:17, one launch (start us, length us, event | category | flops | bytes accessed | tf_op | source)
XLA Modules:
  0.0 157.3 jit_solution(14838128526364496584)
XLA Ops:
  0.6 153.8 %bucket_pass.1 = (f32[1024,256]{1,0:T(8,128)}, f32[8,128]{1,0:T(8,128)}) custom-call(f32[1024,256]{1,0:T(8,128)} %table_in.1, f32[8,128]{1,0:T(8,128)} %bitcast.3, f32[4,256]{1,0:T(4,128)} %relations_in.1, s32[2,1024]{1,0:T(2,128)} %src_in.1, s32[2,1024]{1,0:T(2,128)} %rel_in.1, s32[2,1024]{1,0:T(2,128)} %dst_in.1, s32[1,2]{1,0:T(1,128)} %bitcast.5, ...), custom_call_target="tpu_custom_call" | custom-call | tf_op jit(solution)/shard_map/bucket_pass/pallas_call | solution.py:311
  154.4 0.0 copy-start
  154.4 2.3 %copy.12 = f32[1024,256]{1,0:T(8,128)} copy(f32[1024,256]{1,0:T(8,128)} %get-tuple-element.8) | data formatting | bytes 2097152
  156.7 0.0 copy-done
  156.7 0.6 copy.13
Async XLA Ops:
  154.4 2.3 %copy-start = (f32[8,128]{1,0:T(8,128)S(1)}, f32[8,128]{1,0:T(8,128)}, u32[]{:S(2)}) copy-start(f32[8,128]{1,0:T(8,128)} %get-tuple-element.5) | copy-start | bytes 12292

commit v4 on v3

--- a/solution.py
+++ b/solution.py
@@ -16,12 +16,13 @@
 ROWS, DIM = 1024, 256
 EDGES, FETCH = 1024, 2048
 CAP = FETCH // PEERS
-STEP = 256
+STEP = 128
 SLOTS = STEP // CAP
 STEPS = FETCH // STEP
+PER = NZ // SLOTS
 TILE = 256
-LEADS = (3, 3)
-LAGS = (5, 0)
+LEADS = (6, 6)
+LAGS = (11, 0)
 BF16, F32 = jnp.bfloat16, jnp.float32
 
 
@@ -196,21 +197,23 @@
             packed[b, i : i + 1, :] = row
 
         def push_served(i):
+            a, half = i // PER, i % PER * SLOTS
             for m in range(SLOTS):
                 j = i * SLOTS + m
                 send(
-                    rows_of(served.at[b], j), rows_of(fetched.at[b], j), serve_sent.at[b], serve_here.at[b, i], ahead, toward(i, m)
+                    rows_of(served.at[b], j), rows_of(fetched.at[b], j), serve_sent.at[b], serve_here.at[b, i], ahead, toward(a, half + m)
                 )
 
         def push_grads(i):
+            a, half = i // PER, i % PER * SLOTS
             for m in range(SLOTS):
                 j = i * SLOTS + m
                 send(
-                    rows_of(gradf.at[b], j), rows_of(returned.at[b], j), return_sent.at[b], return_here.at[b, i], behind, back(i, m)
+                    rows_of(gradf.at[b], j), rows_of(returned.at[b], j), return_sent.at[b], return_here.at[b, i], behind, back(a, half + m)
                 )
 
         def serve(i, carry):
-            ids = [packed[b, pl.ds(2 * i + h, 1), :] for h in range(2)]
+            ids = [packed[b, pl.ds(STEP // 128 * i + h, 1), :] for h in range(STEP // 128)]
             at = pl.ds(pl.multiple_of(i * STEP, STEP), STEP)
             served[b, at, :] = dot(one_hot_rows(ids), split[:, :DIM]).astype(BF16)
 
@@ -274,7 +277,7 @@
         def collect(i, carry):
             at = pl.ds(pl.multiple_of(i * STEP, STEP), STEP)
             landed(returned.at[b, at], return_here.at[b, i])
-            ids = [packed[b, pl.ds(2 * i + h, 1), :] for h in range(2)]
+            ids = [packed[b, pl.ds(STEP // 128 * i + h, 1), :] for h in range(STEP // 128)]
             back_rows = returned[b, at, :]
             for t in range(ROWS // TILE):
                 spot = slice(t * TILE, (t + 1) * TILE)

time: 157 us -> 153 us (0.975)
  the two profiles are of different devices: /device:TPU:17 before, /device:TPU:1 now
where the time goes in v4:
time: 153 us
  Pallas kernels  149 us (97%)
  local copies, waits for them, and re-layouts  2.86 us (2%)
    pallas_call x1, Pallas kernels, on_device(): pl.pallas_call(functools.partial(kernel, offsets), out_shape=(jax.ShapeDt...  149 us

profile of v4, /device:TPU:1, one launch (start us, length us, event | category | flops | bytes accessed | tf_op | source)
XLA Modules:
  0.0 152.5 jit_solution(1854551064768242987)
XLA Ops:
  0.6 149.0 %bucket_pass.1 = (f32[1024,256]{1,0:T(8,128)}, f32[8,128]{1,0:T(8,128)}) custom-call(f32[1024,256]{1,0:T(8,128)} %table_in.1, f32[8,128]{1,0:T(8,128)} %bitcast.3, f32[4,256]{1,0:T(4,128)} %relations_in.1, s32[2,1024]{1,0:T(2,128)} %src_in.1, s32[2,1024]{1,0:T(2,128)} %rel_in.1, s32[2,1024]{1,0:T(2,128)} %dst_in.1, s32[1,2]{1,0:T(1,128)} %bitcast.5, ...), custom_call_target="tpu_custom_call" | custom-call | tf_op jit(solution)/shard_map/bucket_pass/pallas_call | solution.py:314
  149.7 0.0 copy-start
  149.7 2.3 %copy.12 = f32[1024,256]{1,0:T(8,128)} copy(f32[1024,256]{1,0:T(8,128)} %get-tuple-element.8) | data formatting | bytes 2097152
  151.9 0.0 copy-done
  152.0 0.6 copy.13
Async XLA Ops:
  149.7 2.3 %copy-start = (f32[8,128]{1,0:T(8,128)S(1)}, f32[8,128]{1,0:T(8,128)}, u32[]{:S(2)}) copy-start(f32[8,128]{1,0:T(8,128)} %get-tuple-element.5) | copy-start | bytes 12292
